TPU v7x, 32 devices: a whole 2x2x4 slice. The times are simulated.
32 devices in a mesh: rep: 2 (over x), gx: 8 (over z, y), gy: 2 (over core).
Axes of the slice: x: 2, y: 2, z: 4, core: 2. Of those that a mesh axis runs over, the one named last changes fastest.
Arguments:
- tokens: bfloat16 [4, 128, 9216], P(None, ('rep', 'gx'), 'gy'), parts along dimension 1, may hold values from -6 to 6
- weight_in: bfloat16 [9216, 4096], P('gy', 'gx'), may hold values from -0.0625 to 0.0625
- weight_out: bfloat16 [4096, 9216], P('gx', 'gy'), may hold values from -0.09375 to 0.09375
Outputs:
- outputs: bfloat16 [4, 128, 9216], P(None, ('rep', 'gx'), 'gy'), parts along dimension 1
There are 2 independent parts, one for each index of `rep`. A program takes and returns all parts, laid end to end along the dimension named above; an argument that names none is the same for every part. Nothing has to cross between parts.
All inputs are finite; a program needn't handle non-finite values.
Results may differ from a plain program's by a relative error of at most 0.023.
Values may be sent and summed in bfloat16 or wider, within the bound.
A program may use at most 64 MiB of HBM per device.

v0:
```python
import jax
import jax.numpy as jnp
from jax import lax
from jax.sharding import PartitionSpec as P


def one_step(step_rows, weight_in, weight_out):
    partial_pre = jnp.dot(
        lax.all_gather(step_rows, "gx", axis=0, tiled=True),
        weight_in,
        preferred_element_type=jnp.float32,
    )
    pre = lax.psum(partial_pre.astype(jnp.bfloat16), "gy").astype(jnp.float32)
    hidden = jax.nn.gelu(pre, approximate=False).astype(jnp.bfloat16)
    return lax.psum_scatter(
        jnp.dot(hidden, weight_out, preferred_element_type=jnp.float32).astype(jnp.bfloat16),
        "gx",
        scatter_dimension=0,
        tiled=True,
    )


def on_device(tokens, weight_in, weight_out):
    results = []
    previous = None
    for step in range(tokens.shape[0]):
        if previous is None:
            inputs = tokens[step]
        else:
            inputs = (tokens[step].astype(jnp.float32) + previous.astype(jnp.float32)).astype(
                jnp.bfloat16
            )
        previous = one_step(inputs, weight_in, weight_out)
        results.append(previous)
    return jnp.stack(results, 0)


def solution(mesh):
    return jax.shard_map(
        on_device,
        mesh=mesh,
        in_specs=(P(None, ("rep", "gx"), "gy"), P("gy", "gx"), P("gx", "gy")),
        out_specs=P(None, ("rep", "gx"), "gy"),
        check_vma=False,
    )
```

profile of v0, /device:TPU:0, one launch (start us, length us, event | category | flops | bytes accessed | tf_op | source)
XLA Modules:
  0.0 503.3 jit_solution(14710544362029461353)
XLA Ops:
  7.4 33.2 %all-gather = bf16[1,64,4608]{2,1,0:T(8,128)(2,1)S(1)} all-gather(bf16[1,8,4608]{2,1,0:T(8,128)(2,1)S(1)} %slice.12), channel_id=2, replica_groups=mesh['rep'=2,'gx'=8,'gy'=2] {'gx'}, dimensions={1}, use_global_device_ids=true | all-gather | bytes 663552 | tf_op jit(solution)/shard_map/all_gather | solution.py:9
  40.6 3.9 convolution_convert_fusion.7
  44.6 18.9 %all-reduce.5.cloned.1.call-done = bf16[64,512]{1,0:T(8,128)(2,1)} async-done(((bf16[64,512]{1,0:T(8,128)(2,1)}), bf16[64,512]{1,0:T(8,128)(2,1)}) %all-reduce.5.cloned.1.call-update) | async-done | bytes 65552 | tf_op jit(solution)/shard_map/psum | solution.py:13
  63.5 4.3 convolution_convert_fusion.3
  67.9 63.4 %reduce-scatter.5.cloned.1.call-done = bf16[8,4608]{1,0:T(8,128)(2,1)} async-done(((bf16[64,4608]{1,0:T(8,128)(2,1)}), bf16[8,4608]{1,0:T(8,128)(2,1)}) %reduce-scatter.5.cloned.1.call-update) | async-done | bytes 73744 | tf_op jit(solution)/shard_map/reduce_scatter | solution.py:15
  131.3 0.9 fusion.3
  132.2 31.7 %all_gather.13 = bf16[64,4608]{1,0:T(8,128)(2,1)S(1)} all-gather(bf16[8,4608]{1,0:T(8,128)(2,1)S(1)} %fusion.3), channel_id=1, replica_groups=mesh['rep'=2,'gx'=8,'gy'=2] {'gx'}, dimensions={0}, use_global_device_ids=true | all-gather | bytes 663552 | tf_op jit(solution)/shard_map/all_gather | solution.py:9
  163.9 3.9 convolution_convert_fusion.6
  167.8 16.9 %all-reduce.7.cloned.1.call-done = bf16[64,512]{1,0:T(8,128)(2,1)} async-done(((bf16[64,512]{1,0:T(8,128)(2,1)}), bf16[64,512]{1,0:T(8,128)(2,1)}) %all-reduce.7.cloned.1.call-update) | async-done | bytes 65552 | tf_op jit(solution)/shard_map/psum | solution.py:13
  184.7 4.3 convolution_convert_fusion.2
  189.1 63.4 %reduce-scatter.7.cloned.1.call-done = bf16[8,4608]{1,0:T(8,128)(2,1)} async-done(((bf16[64,4608]{1,0:T(8,128)(2,1)}), bf16[8,4608]{1,0:T(8,128)(2,1)}) %reduce-scatter.7.cloned.1.call-update) | async-done | bytes 73744 | tf_op jit(solution)/shard_map/reduce_scatter | solution.py:15
  252.5 0.9 fusion.2
  253.4 31.6 %all_gather.14 = bf16[64,4608]{1,0:T(8,128)(2,1)S(1)} all-gather(bf16[8,4608]{1,0:T(8,128)(2,1)S(1)} %fusion.2), channel_id=1, replica_groups=mesh['rep'=2,'gx'=8,'gy'=2] {'gx'}, dimensions={0}, use_global_device_ids=true | all-gather | bytes 663552 | tf_op jit(solution)/shard_map/all_gather | solution.py:9
  285.0 3.9 convolution_convert_fusion.5
  288.9 16.9 %all-reduce.9.cloned.1.call-done = bf16[64,512]{1,0:T(8,128)(2,1)} async-done(((bf16[64,512]{1,0:T(8,128)(2,1)}), bf16[64,512]{1,0:T(8,128)(2,1)}) %all-reduce.9.cloned.1.call-update) | async-done | bytes 65552 | tf_op jit(solution)/shard_map/psum | solution.py:13
  305.9 4.3 convolution_convert_fusion.1
  310.3 63.4 %reduce-scatter.9.cloned.1.call-done = bf16[8,4608]{1,0:T(8,128)(2,1)} async-done(((bf16[64,4608]{1,0:T(8,128)(2,1)}), bf16[8,4608]{1,0:T(8,128)(2,1)}) %reduce-scatter.9.cloned.1.call-update) | async-done | bytes 73744 | tf_op jit(solution)/shard_map/reduce_scatter | solution.py:15
  373.6 0.9 fusion.1
  374.5 31.7 %all_gather.15 = bf16[64,4608]{1,0:T(8,128)(2,1)S(1)} all-gather(bf16[8,4608]{1,0:T(8,128)(2,1)S(1)} %fusion.1), channel_id=1, replica_groups=mesh['rep'=2,'gx'=8,'gy'=2] {'gx'}, dimensions={0}, use_global_device_ids=true | all-gather | bytes 663552 | tf_op jit(solution)/shard_map/all_gather | solution.py:9
  406.2 3.9 convolution_convert_fusion.4
  410.2 16.9 %all-reduce.11.cloned.1.call-done = bf16[64,512]{1,0:T(8,128)(2,1)} async-done(((bf16[64,512]{1,0:T(8,128)(2,1)}), bf16[64,512]{1,0:T(8,128)(2,1)}) %all-reduce.11.cloned.1.call-update) | async-done | bytes 65552 | tf_op jit(solution)/shard_map/psum | solution.py:13
  427.1 4.3 convolution_convert_fusion
  431.4 63.4 %reduce-scatter.11.cloned.1.call-done = bf16[8,4608]{1,0:T(8,128)(2,1)} async-done(((bf16[64,4608]{1,0:T(8,128)(2,1)}), bf16[8,4608]{1,0:T(8,128)(2,1)}) %reduce-scatter.11.cloned.1.call-update) | async-done | bytes 73744 | tf_op jit(solution)/shard_map/reduce_scatter | solution.py:15
  494.9 1.6 pad_maximum_fusion
  (25 shorter events, 1.3 us)
Async XLA Ops:
  6.5 56.9 %all-reduce.5.cloned.1.call-start = ((), (), s32[]{:S(2)}) async-start(), calls=%async_computation.4 | async-start | bytes 131072 | tf_op jit(solution)/shard_map/psum | solution.py:13
  44.5 86.7 %copy-start.3 = (bf16[4,8,4608]{2,1,0:T(8,128)(2,1)S(1)}, bf16[4,8,4608]{2,1,0:T(8,128)(2,1)}, u32[]{:S(2)}) copy-start(bf16[4,8,4608]{2,1,0:T(8,128)(2,1)} %param.3) | copy-start | bytes 884740
  44.6 86.7 %reduce-scatter.5.cloned.1.call-start = ((), (), s32[]{:S(2)}) async-start(), calls=%async_computation.5 | async-start | bytes 663552 | tf_op jit(solution)/shard_map/reduce_scatter | solution.py:15
  67.8 116.9 %all-reduce.7.cloned.1.call-start = ((), (), s32[]{:S(2)}) async-start(), calls=%async_computation.6 | async-start | bytes 131072 | tf_op jit(solution)/shard_map/psum | solution.py:13
  167.8 84.7 %reduce-scatter.7.cloned.1.call-start = ((), (), s32[]{:S(2)}) async-start(), calls=%async_computation.7 | async-start | bytes 663552 | tf_op jit(solution)/shard_map/reduce_scatter | solution.py:15
  189.1 116.8 %all-reduce.9.cloned.1.call-start = ((), (), s32[]{:S(2)}) async-start(), calls=%async_computation.8 | async-start | bytes 131072 | tf_op jit(solution)/shard_map/psum | solution.py:13
  288.9 84.8 %reduce-scatter.9.cloned.1.call-start = ((), (), s32[]{:S(2)}) async-start(), calls=%async_computation.9 | async-start | bytes 663552 | tf_op jit(solution)/shard_map/reduce_scatter | solution.py:15
  310.2 116.8 %all-reduce.11.cloned.1.call-start = ((), (), s32[]{:S(2)}) async-start(), calls=%async_computation.10 | async-start | bytes 131072 | tf_op jit(solution)/shard_map/psum | solution.py:13
  410.1 84.7 %copy-start = (bf16[8,4608]{1,0:T(8,128)(2,1)S(1)}, bf16[8,4608]{1,0:T(8,128)(2,1)}, u32[]{:S(2)}) copy-start(bf16[8,4608]{1,0:T(8,128)(2,1)} %reduce-scatter.5.cloned.1.call-done) | copy-start | bytes 221188
  410.1 84.7 %copy-start.1 = (bf16[8,4608]{1,0:T(8,128)(2,1)S(1)}, bf16[8,4608]{1,0:T(8,128)(2,1)}, u32[]{:S(2)}) copy-start(bf16[8,4608]{1,0:T(8,128)(2,1)} %reduce-scatter.7.cloned.1.call-done) | copy-start | bytes 221188
  410.1 84.7 %copy-start.2 = (bf16[8,4608]{1,0:T(8,128)(2,1)S(1)}, bf16[8,4608]{1,0:T(8,128)(2,1)}, u32[]{:S(2)}) copy-start(bf16[8,4608]{1,0:T(8,128)(2,1)} %reduce-scatter.9.cloned.1.call-done) | copy-start | bytes 221188
  410.2 84.7 %reduce-scatter.11.cloned.1.call-start = ((), (), s32[]{:S(2)}) async-start(), calls=%async_computation.11 | async-start | bytes 663552 | tf_op jit(solution)/shard_map/reduce_scatter | solution.py:15
Sparse Core Ops, SparseCore 0:
  44.7 18.7 all-reduce.4
  67.9 63.2 reduce-scatter.4
  167.9 16.7 all-reduce.6
  189.2 63.2 reduce-scatter.6
  289.0 16.8 all-reduce.8
  310.3 63.2 reduce-scatter.8
  410.3 16.7 all-reduce.10
  431.5 63.2 reduce-scatter.10
where the time goes:
time: 504 us; the launch traced here: 503 us
  waiting for transfers between devices  323 us (64%)
  blocking collectives  128 us (25%)
  matrix products  32.9 us (7%)
  between operations  13.5 us (3%)
    reduce_scatter x4, waiting for transfers between devices, one_step(): lax.psum_scatter(jnp.dot(hidden, weight_out, preferred_element_type=jnp.f...  254 us
    all_gather x4, blocking collectives, one_step(): lax.all_gather(step_rows, 'gx', axis=0, tiled=True)  128 us
    psum x4, waiting for transfers between devices, one_step(): pre = lax.psum(partial_pre.astype(jnp.bfloat16), 'gy').astype(jnp.float32)  69.5 us
    dot_general x4, matrix products, one_step(): jnp.dot(hidden, weight_out, preferred_element_type=jnp.float32)  17.3 us
    dot_general x4, matrix products, one_step(): jnp.dot(lax.all_gather(step_rows, 'gx', axis=0, tiled=True), weight_in, p...  15.6 us
  transfers between devices with their start and end apart: 8, of which 8 were waited for; matrix products, arithmetic and copies ran while one was open for 0% of the time, Pallas kernels for 0%

commit v1 on v0

v1 whole, which is shorter than its diff:
```python
import functools

import jax
import jax.numpy as jnp
from jax import lax
from jax.experimental import pallas as pl
from jax.experimental.pallas import tpu as pltpu
from jax.sharding import PartitionSpec as P

MESH = pl.DeviceIdType.MESH
CHUNKS = 3
NEAR = 2


def gelu(x):
    return 0.5 * x * (1.0 + lax.erf(x * 0.7071067811865476))


def kernel(
    n, tok, w_in, w_out, out,
    win, wout, acc, hid, mine, xg, ps, pr, sy, ry, sz, rz,
    win_sem, wout_sem, agz_s, agz_r, agy_s, agy_r, p_s, p_r, rsy_s, rsy_r, rsz_s, rsz_r,
):
    steps, rows, d = tok.shape
    nz = n // NEAR
    width = d // CHUNKS
    gx = lax.axis_index("gx")
    gy = lax.axis_index("gy")
    y, z = lax.rem(gx, NEAR), lax.div(gx, NEAR)
    y_peer = {"gx": z * NEAR + (1 - y)}
    core_peer = {"gy": 1 - gy}

    def z_at(j):
        return lax.rem(z + j, nz)

    def z_id(zz):
        return {"gx": zz * NEAR + y}

    def cols(c):
        return pl.ds(c * width, width)

    def win_copy(c):
        return pltpu.make_async_copy(w_in.at[cols(c), :], win.at[cols(c), :], win_sem.at[c])

    def wout_copy(c):
        return pltpu.make_async_copy(w_out.at[:, cols(c)], wout.at[:, cols(c)], wout_sem.at[c])

    def remote(src, dst, s_sem, r_sem, to):
        return pltpu.make_async_remote_copy(
            src_ref=src, dst_ref=dst, send_sem=s_sem, recv_sem=r_sem, device_id=to, device_id_type=MESH
        )

    def ag_z(s, c, zz):
        return remote(xg.at[s, c, 0, z], xg.at[s, c, 0, z], agz_s.at[s, c, zz], agz_r.at[s, c, z], z_id(zz))

    def ag_z_in(s, c, zz):
        return remote(xg.at[s, c, 0, zz], xg.at[s, c, 0, zz], agz_s.at[s, c, zz], agz_r.at[s, c, zz], z_id(zz))

    def ag_y(s, c, zz):
        return remote(xg.at[s, c, 0, zz], xg.at[s, c, 1, zz], agy_s.at[s, c, zz], agy_r.at[s, c, zz], y_peer)

    def psum(s):
        return remote(ps.at[s], pr.at[s], p_s.at[s], p_r.at[s], core_peer)

    def rs_y(s, c):
        return remote(sy.at[s, c], ry.at[s, c], rsy_s.at[s, c], rsy_r.at[s, c], y_peer)

    def rs_z(s, c, zz):
        return remote(sz.at[s, c, zz], rz.at[s, c, z], rsz_s.at[s, c, zz], rsz_r.at[s, c, z], z_id(zz))

    def rs_z_in(s, c, zz):
        return remote(sz.at[s, c, zz], rz.at[s, c, zz], rsz_s.at[s, c, zz], rsz_r.at[s, c, zz], z_id(zz))

    for c in range(CHUNKS):
        win_copy(c).start()
    for c in range(CHUNKS):
        wout_copy(c).start()

    barrier = pltpu.get_barrier_semaphore()
    pl.semaphore_signal(barrier, inc=1, device_id=y_peer, device_id_type=MESH)
    pl.semaphore_signal(barrier, inc=1, device_id=core_peer, device_id_type=MESH)
    for j in range(1, nz):
        pl.semaphore_signal(barrier, inc=1, device_id=z_id(z_at(j)), device_id_type=MESH)
    pl.semaphore_wait(barrier, nz + 1)

    def send_inputs(s, c):
        ag_y(s, c, z).start()
        for j in range(1, nz):
            ag_z(s, c, z_at(j)).start()

    for c in range(CHUNKS):
        xg[0, c, 0, z] = tok[0, :, cols(c)]
        send_inputs(0, c)
    for c in range(CHUNKS):
        win_copy(c).wait()

    def step(s, carry):
        def project(c):
            for j in range(nz):
                ag_y(s, c, z_at(j)).wait_recv()
            part = jnp.dot(
                xg[s, c].reshape(n * rows, width), win[cols(c), :], preferred_element_type=jnp.float32
            )
            acc[...] = part if c == 0 else acc[...] + part

        for c in range(CHUNKS):
            for j in range(1, nz):
                zz = z_at(j)
                ag_z_in(s, c, zz).wait_recv()
                ag_y(s, c, zz).start()
            if c:
                project(c - 1)
        project(CHUNKS - 1)

        ps[s] = acc[...].astype(jnp.bfloat16)
        psum(s).start()

        @pl.when(s == 0)
        def _():
            for c in range(CHUNKS):
                wout_copy(c).wait()

        psum(s).wait_recv()
        hid[...] = gelu(acc[...] + pr[s].astype(jnp.float32)).astype(jnp.bfloat16)

        def pair_sum(c):
            rs_y(s, c).wait_recv()
            for j in range(1, nz):
                zz = z_at(j)
                sz[s, c, zz] = (mine[c, zz] + ry[s, c, zz].astype(jnp.float32)).astype(jnp.bfloat16)
                rs_z(s, c, zz).start()
            mine[c, z] = mine[c, z] + ry[s, c, z].astype(jnp.float32)

        for c in range(CHUNKS):
            terms = jnp.dot(hid[...], wout[:, cols(c)], preferred_element_type=jnp.float32)
            terms = terms.reshape(NEAR, nz, rows, width)
            sy[s, c] = terms[1].astype(jnp.bfloat16)
            rs_y(s, c).start()
            mine[c] = terms[0]
            if c:
                pair_sum(c - 1)
        pair_sum(CHUNKS - 1)

        for c in range(CHUNKS):
            total = mine[c, z]
            for j in range(1, nz):
                zz = z_at(j)
                rs_z_in(s, c, zz).wait_recv()
                total = total + rz[s, c, zz].astype(jnp.float32)
            result = total.astype(jnp.bfloat16)
            out[s, :, cols(c)] = result

            @pl.when(s < steps - 1)
            def _():
                nxt = tok[s + 1, :, cols(c)].astype(jnp.float32) + result.astype(jnp.float32)
                xg[s + 1, c, 0, z] = nxt.astype(jnp.bfloat16)
                send_inputs(s + 1, c)

        for c in range(CHUNKS):
            ag_y(s, c, z).wait_send()
            rs_y(s, c).wait_send()
            for j in range(1, nz):
                zz = z_at(j)
                ag_y(s, c, zz).wait_send()
                ag_z(s, c, zz).wait_send()
                rs_z(s, c, zz).wait_send()
        psum(s).wait_send()
        return carry

    lax.fori_loop(0, steps, step, 0)


def on_device(n, tokens, weight_in, weight_out):
    steps, rows, d = tokens.shape
    ff = weight_in.shape[1]
    nz = n // NEAR
    width = d // CHUNKS
    bf16, f32 = jnp.bfloat16, jnp.float32
    dma = pltpu.SemaphoreType.DMA
    flops = steps * n * rows * d * ff * 4
    return pl.pallas_call(
        functools.partial(kernel, n),
        out_shape=jax.ShapeDtypeStruct(tokens.shape, bf16),
        in_specs=[
            pl.BlockSpec(memory_space=pltpu.VMEM),
            pl.BlockSpec(memory_space=pl.ANY),
            pl.BlockSpec(memory_space=pl.ANY),
        ],
        out_specs=pl.BlockSpec(memory_space=pltpu.VMEM),
        scratch_shapes=[
            pltpu.VMEM((d, ff), bf16),
            pltpu.VMEM((ff, d), bf16),
            pltpu.VMEM((n * rows, ff), f32),
            pltpu.VMEM((n * rows, ff), bf16),
            pltpu.VMEM((CHUNKS, nz, rows, width), f32),
            pltpu.VMEM((steps, CHUNKS, NEAR, nz, rows, width), bf16),
            pltpu.VMEM((steps, n * rows, ff), bf16),
            pltpu.VMEM((steps, n * rows, ff), bf16),
            pltpu.VMEM((steps, CHUNKS, nz, rows, width), bf16),
            pltpu.VMEM((steps, CHUNKS, nz, rows, width), bf16),
            pltpu.VMEM((steps, CHUNKS, nz, rows, width), bf16),
            pltpu.VMEM((steps, CHUNKS, nz, rows, width), bf16),
            dma((CHUNKS,)),
            dma((CHUNKS,)),
            dma((steps, CHUNKS, nz)),
            dma((steps, CHUNKS, nz)),
            dma((steps, CHUNKS, nz)),
            dma((steps, CHUNKS, nz)),
            dma((steps,)),
            dma((steps,)),
            dma((steps, CHUNKS)),
            dma((steps, CHUNKS)),
            dma((steps, CHUNKS, nz)),
            dma((steps, CHUNKS, nz)),
        ],
        compiler_params=pltpu.CompilerParams(
            collective_id=0, has_side_effects=True, vmem_limit_bytes=60 * 1024 * 1024
        ),
        cost_estimate=pl.CostEstimate(
            flops=flops, bytes_accessed=4 * d * ff, transcendentals=steps * n * rows * ff
        ),
    )(tokens, weight_in, weight_out)


def solution(mesh):
    return jax.shard_map(
        functools.partial(on_device, mesh.shape["gx"]),
        mesh=mesh,
        in_specs=(P(None, ("rep", "gx"), "gy"), P("gy", "gx"), P("gx", "gy")),
        out_specs=P(None, ("rep", "gx"), "gy"),
        check_vma=False,
    )
```

time: 504 us -> 113 us (0.22)
  waiting for transfers between devices: 323 us -> 0 us
  blocking collectives: 128 us -> 0 us
  Pallas kernels: 0 us -> 111 us
  matrix products: 32.9 us -> 0 us
  between operations: 13.5 us -> 0.01 us
    reduce_scatter x4 -> x0, waiting for transfers between devices: 254 us -> none  [one_step(): lax.psum_scatter(jnp.dot(hidden, weight_out, preferred_element_type=jnp.f...]
    all_gather x4 -> x0, blocking collectives: 128 us -> none  [one_step(): lax.all_gather(step_rows, 'gx', axis=0, tiled=True)]
    pallas_call x0 -> x1, Pallas kernels: none -> 111 us  [on_device(): pl.pallas_call(functools.partial(kernel, n), out_shape=jax.ShapeDtypeStru...]
    psum x4 -> x0, waiting for transfers between devices: 69.5 us -> none  [one_step(): pre = lax.psum(partial_pre.astype(jnp.bfloat16), 'gy').astype(jnp.float32)]
    dot_general x8 -> x0, matrix products: 32.9 us -> none  [the longest x4 17.3 us: one_step(): jnp.dot(hidden, weight_out, preferred_element_type=jnp.float32)]
  transfers between devices with their start and end apart: 8 -> 0, of which waited for: 8 -> 0; matrix products, arithmetic and copies ran while one was open for 0% -> 0% of each run, Pallas kernels for 0% -> 0%
where the time goes in v1:
time: 113 us; the launch traced here: 112 us
  Pallas kernels  111 us (98%)
  local copies, waits for them, and re-layouts  1.69 us (1%)
    pallas_call x1, Pallas kernels, on_device(): pl.pallas_call(functools.partial(kernel, n), out_shape=jax.ShapeDtypeStru...  111 us

profile of v1, /device:TPU:0, one launch (start us, length us, event | category | flops | bytes accessed | tf_op | source)
XLA Modules:
  0.0 112.4 jit_solution(16638133484748651303)
XLA Ops:
  0.0 110.7 %shard_map.37 = bf16[4,8,4608]{2,1,0:T(8,128)(2,1)} custom-call(bf16[4,8,4608]{2,1,0:T(8,128)(2,1)} %tok.1, bf16[4608,512]{1,0:T(8,128)(2,1)} %w_in.1, bf16[512,4608]{1,0:T(8,128)(2,1)} %w_out.1), custom_call_target="tpu_custom_call" | custom-call | flops 2415919104 | bytes 9437184 | tf_op jit(solution)/shard_map/pallas_call | solution.py:181
  110.7 1.7 %copy.5 = bf16[4,8,4608]{2,1,0:T(8,128)(2,1)} copy(bf16[4,8,4608]{2,1,0:T(8,128)(2,1)} %shard_map.37) | data formatting | bytes 589824

commit v2 on v1

--- a/solution.py
+++ b/solution.py
@@ -8,7 +8,7 @@
 from jax.sharding import PartitionSpec as P
 
 MESH = pl.DeviceIdType.MESH
-CHUNKS = 3
+CHUNKS = 2
 NEAR = 2
 
 
@@ -62,8 +62,8 @@
     def psum(s):
         return remote(ps.at[s], pr.at[s], p_s.at[s], p_r.at[s], core_peer)
 
-    def rs_y(s, c):
-        return remote(sy.at[s, c], ry.at[s, c], rsy_s.at[s, c], rsy_r.at[s, c], y_peer)
+    def rs_y(s, c, zz):
+        return remote(sy.at[s, c, zz], ry.at[s, c, zz], rsy_s.at[s, c, zz], rsy_r.at[s, c, zz], y_peer)
 
     def rs_z(s, c, zz):
         return remote(sz.at[s, c, zz], rz.at[s, c, z], rsz_s.at[s, c, zz], rsz_r.at[s, c, z], z_id(zz))
@@ -84,9 +84,9 @@
     pl.semaphore_wait(barrier, nz + 1)
 
     def send_inputs(s, c):
+        for j in range(nz - 1, 0, -1):
+            ag_z(s, c, z_at(j)).start()
         ag_y(s, c, z).start()
-        for j in range(1, nz):
-            ag_z(s, c, z_at(j)).start()
 
     for c in range(CHUNKS):
         xg[0, c, 0, z] = tok[0, :, cols(c)]
@@ -124,18 +124,20 @@
         hid[...] = gelu(acc[...] + pr[s].astype(jnp.float32)).astype(jnp.bfloat16)
 
         def pair_sum(c):
-            rs_y(s, c).wait_recv()
-            for j in range(1, nz):
-                zz = z_at(j)
+            for j in range(1, nz):
+                zz = z_at(j)
+                rs_y(s, c, zz).wait_recv()
                 sz[s, c, zz] = (mine[c, zz] + ry[s, c, zz].astype(jnp.float32)).astype(jnp.bfloat16)
                 rs_z(s, c, zz).start()
+            rs_y(s, c, z).wait_recv()
             mine[c, z] = mine[c, z] + ry[s, c, z].astype(jnp.float32)
 
         for c in range(CHUNKS):
             terms = jnp.dot(hid[...], wout[:, cols(c)], preferred_element_type=jnp.float32)
             terms = terms.reshape(NEAR, nz, rows, width)
             sy[s, c] = terms[1].astype(jnp.bfloat16)
-            rs_y(s, c).start()
+            for j in range(nz):
+                rs_y(s, c, z_at((j + 1) % nz)).start()
             mine[c] = terms[0]
             if c:
                 pair_sum(c - 1)
@@ -158,7 +160,8 @@
 
         for c in range(CHUNKS):
             ag_y(s, c, z).wait_send()
-            rs_y(s, c).wait_send()
+            for zz in range(nz):
+                rs_y(s, c, zz).wait_send()
             for j in range(1, nz):
                 zz = z_at(j)
                 ag_y(s, c, zz).wait_send()
@@ -208,8 +211,8 @@
             dma((steps, CHUNKS, nz)),
             dma((steps,)),
             dma((steps,)),
-            dma((steps, CHUNKS)),
-            dma((steps, CHUNKS)),
+            dma((steps, CHUNKS, nz)),
+            dma((steps, CHUNKS, nz)),
             dma((steps, CHUNKS, nz)),
             dma((steps, CHUNKS, nz)),
         ],

time: 113 us -> 104 us (0.920)
  Pallas kernels: 111 us -> 102 us
    pallas_call x1, Pallas kernels: 111 us -> 102 us  [on_device(): pl.pallas_call(functools.partial(kernel, n), out_shape=jax.ShapeDtypeStru...]
where the time goes in v2:
time: 104 us
  Pallas kernels  102 us (98%)
  local copies, waits for them, and re-layouts  1.69 us (2%)
    pallas_call x1, Pallas kernels, on_device(): pl.pallas_call(functools.partial(kernel, n), out_shape=jax.ShapeDtypeStru...  102 us

profile of v2, /device:TPU:0, one launch (start us, length us, event | category | flops | bytes accessed | tf_op | source)
XLA Modules:
  0.0 104.1 jit_solution(8568952431013851861)
XLA Ops:
  0.0 102.4 %shard_map.37 = bf16[4,8,4608]{2,1,0:T(8,128)(2,1)} custom-call(bf16[4,8,4608]{2,1,0:T(8,128)(2,1)} %tok.1, bf16[4608,512]{1,0:T(8,128)(2,1)} %w_in.1, bf16[512,4608]{1,0:T(8,128)(2,1)} %w_out.1), custom_call_target="tpu_custom_call" | custom-call | flops 2415919104 | bytes 9437184 | tf_op jit(solution)/shard_map/pallas_call | solution.py:184
  102.4 1.7 %copy.5 = bf16[4,8,4608]{2,1,0:T(8,128)(2,1)} copy(bf16[4,8,4608]{2,1,0:T(8,128)(2,1)} %shard_map.37) | data formatting | bytes 589824

commit v3 on v2

--- a/solution.py
+++ b/solution.py
@@ -30,8 +30,14 @@
     y_peer = {"gx": z * NEAR + (1 - y)}
     core_peer = {"gy": 1 - gy}
 
+    toward = jnp.where(z < nz // 2, 1, -1)
+    margin = jnp.minimum(z, nz - 1 - z)
+
+    mate = z + 1 - 2 * lax.rem(z, 2)
+
     def z_at(j):
-        return lax.rem(z + j, nz)
+        near = toward * ((j + 1) // 2) * (1 if j % 2 else -1)
+        return z + jnp.where(j <= 2 * margin, near, toward * (j - margin))
 
     def z_id(zz):
         return {"gx": zz * NEAR + y}
@@ -58,6 +64,10 @@
 
     def ag_y(s, c, zz):
         return remote(xg.at[s, c, 0, zz], xg.at[s, c, 1, zz], agy_s.at[s, c, zz], agy_r.at[s, c, zz], y_peer)
+
+    def ag_cross(s, c, zz):
+        to = {"gx": zz * NEAR + (1 - y)}
+        return remote(xg.at[s, c, 0, z], xg.at[s, c, 1, z], agy_s.at[s, c, zz], agy_r.at[s, c, z], to)
 
     def psum(s):
         return remote(ps.at[s], pr.at[s], p_s.at[s], p_r.at[s], core_peer)
@@ -81,21 +91,25 @@
     pl.semaphore_signal(barrier, inc=1, device_id=core_peer, device_id_type=MESH)
     for j in range(1, nz):
         pl.semaphore_signal(barrier, inc=1, device_id=z_id(z_at(j)), device_id_type=MESH)
-    pl.semaphore_wait(barrier, nz + 1)
+    cross = {"gx": mate * NEAR + (1 - y)}
+    pl.semaphore_signal(barrier, inc=1, device_id=cross, device_id_type=MESH)
+    pl.semaphore_wait(barrier, nz + 2)
 
     def send_inputs(s, c):
-        for j in range(nz - 1, 0, -1):
+        for j in range(1, nz):
             ag_z(s, c, z_at(j)).start()
         ag_y(s, c, z).start()
+        ag_cross(s, c, mate).start()
 
     for c in range(CHUNKS):
         xg[0, c, 0, z] = tok[0, :, cols(c)]
         send_inputs(0, c)
-    for c in range(CHUNKS):
-        win_copy(c).wait()
-
     def step(s, carry):
         def project(c):
+            @pl.when(s == 0)
+            def _():
+                win_copy(c).wait()
+
             for j in range(nz):
                 ag_y(s, c, z_at(j)).wait_recv()
             part = jnp.dot(
@@ -107,7 +121,11 @@
             for j in range(1, nz):
                 zz = z_at(j)
                 ag_z_in(s, c, zz).wait_recv()
-                ag_y(s, c, zz).start()
+
+                @pl.when(zz != mate)
+                def _():
+                    ag_y(s, c, zz).start()
+
             if c:
                 project(c - 1)
         project(CHUNKS - 1)
@@ -124,7 +142,7 @@
         hid[...] = gelu(acc[...] + pr[s].astype(jnp.float32)).astype(jnp.bfloat16)
 
         def pair_sum(c):
-            for j in range(1, nz):
+            for j in range(nz - 1, 0, -1):
                 zz = z_at(j)
                 rs_y(s, c, zz).wait_recv()
                 sz[s, c, zz] = (mine[c, zz] + ry[s, c, zz].astype(jnp.float32)).astype(jnp.bfloat16)
@@ -136,8 +154,8 @@
             terms = jnp.dot(hid[...], wout[:, cols(c)], preferred_element_type=jnp.float32)
             terms = terms.reshape(NEAR, nz, rows, width)
             sy[s, c] = terms[1].astype(jnp.bfloat16)
-            for j in range(nz):
-                rs_y(s, c, z_at((j + 1) % nz)).start()
+            for j in range(nz - 1, -1, -1):
+                rs_y(s, c, z_at(j)).start()
             mine[c] = terms[0]
             if c:
                 pair_sum(c - 1)

time: 104 us -> 102 us (0.981)
  Pallas kernels: 102 us -> 99.7 us
    pallas_call x1, Pallas kernels: 102 us -> 99.7 us  [on_device(): pl.pallas_call(functools.partial(kernel, n), out_shape=jax.ShapeDtypeStru...]
where the time goes in v3:
time: 102 us; the launch traced here: 101 us
  Pallas kernels  99.7 us (98%)
  local copies, waits for them, and re-layouts  1.69 us (2%)
    pallas_call x1, Pallas kernels, on_device(): pl.pallas_call(functools.partial(kernel, n), out_shape=jax.ShapeDtypeStru...  99.7 us

profile of v3, /device:TPU:0, one launch (start us, length us, event | category | flops | bytes accessed | tf_op | source)
XLA Modules:
  0.0 101.4 jit_solution(18392711563983715793)
XLA Ops:
  0.0 99.7 %shard_map.37 = bf16[4,8,4608]{2,1,0:T(8,128)(2,1)} custom-call(bf16[4,8,4608]{2,1,0:T(8,128)(2,1)} %tok.1, bf16[4608,512]{1,0:T(8,128)(2,1)} %w_in.1, bf16[512,4608]{1,0:T(8,128)(2,1)} %w_out.1), custom_call_target="tpu_custom_call" | custom-call | flops 2415919104 | bytes 9437184 | tf_op jit(solution)/shard_map/pallas_call | solution.py:202
  99.7 1.7 %copy.5 = bf16[4,8,4608]{2,1,0:T(8,128)(2,1)} copy(bf16[4,8,4608]{2,1,0:T(8,128)(2,1)} %shard_map.37) | data formatting | bytes 589824

commit v4 on v3

--- a/solution.py
+++ b/solution.py
@@ -147,8 +147,6 @@
                 rs_y(s, c, zz).wait_recv()
                 sz[s, c, zz] = (mine[c, zz] + ry[s, c, zz].astype(jnp.float32)).astype(jnp.bfloat16)
                 rs_z(s, c, zz).start()
-            rs_y(s, c, z).wait_recv()
-            mine[c, z] = mine[c, z] + ry[s, c, z].astype(jnp.float32)
 
         for c in range(CHUNKS):
             terms = jnp.dot(hid[...], wout[:, cols(c)], preferred_element_type=jnp.float32)
@@ -162,7 +160,8 @@
         pair_sum(CHUNKS - 1)
 
         for c in range(CHUNKS):
-            total = mine[c, z]
+            rs_y(s, c, z).wait_recv()
+            total = mine[c, z] + ry[s, c, z].astype(jnp.float32)
             for j in range(1, nz):
                 zz = z_at(j)
                 rs_z_in(s, c, zz).wait_recv()

time: 102 us -> 102 us (level)
  no operation moved by 1% of the time
where the time goes in v4:
time: 102 us
  Pallas kernels  99.8 us (98%)
  local copies, waits for them, and re-layouts  1.69 us (2%)
    pallas_call x1, Pallas kernels, on_device(): pl.pallas_call(functools.partial(kernel, n), out_shape=jax.ShapeDtypeStru...  99.8 us

profile of v4, /device:TPU:0, one launch (start us, length us, event | category | flops | bytes accessed | tf_op | source)
XLA Modules:
  0.0 101.5 jit_solution(11805069231221537823)
XLA Ops:
  0.0 99.8 %shard_map.37 = bf16[4,8,4608]{2,1,0:T(8,128)(2,1)} custom-call(bf16[4,8,4608]{2,1,0:T(8,128)(2,1)} %tok.1, bf16[4608,512]{1,0:T(8,128)(2,1)} %w_in.1, bf16[512,4608]{1,0:T(8,128)(2,1)} %w_out.1), custom_call_target="tpu_custom_call" | custom-call | flops 2415919104 | bytes 9437184 | tf_op jit(solution)/shard_map/pallas_call | solution.py:201
  99.8 1.7 %copy.5 = bf16[4,8,4608]{2,1,0:T(8,128)(2,1)} copy(bf16[4,8,4608]{2,1,0:T(8,128)(2,1)} %shard_map.37) | data formatting | bytes 589824
